TPU v7x, 256 devices: a whole 4x4x8 slice. The times are simulated.
256 devices in a mesh: enc: 16 (over x, y), blk: 16 (over z, core).
Axes of the slice: x: 4, y: 4, z: 8, core: 2. Of those that a mesh axis runs over, the one named last changes fastest.
Arguments:
- observations: bfloat16 [131072, 128], P(('enc', 'blk')), may hold values from -6 to 6
- lon_index: int32 [256, 512], P(('enc', 'blk')), may hold values from 0 to 1439
- live_count: int32 [256, 256], P(('enc', 'blk')), may hold values from 0 to 2, as said below
- w_in: bfloat16 [128, 512], replicated, may hold values from -0.5 to 0.5
- w_out: bfloat16 [512, 512], replicated, may hold values from -0.25 to 0.25
- w_spec: float32 [256, 512], replicated, may hold values from -4 to 4
- north: float32 [256, 512], P(('enc', 'blk')), may hold values from -0.8 to 0.8
- south: float32 [256, 512], P(('enc', 'blk')), may hold values from -0.8 to 0.8
- w_mix: bfloat16 [512, 512], replicated, may hold values from -0.25 to 0.25
- loss_sensitivity: bfloat16 [256, 1440, 512], P(('enc', 'blk')), may hold values from -6 to 6
Outputs:
- predicted_state: bfloat16 [256, 1440, 512], P(('enc', 'blk'))
- entry_matrix_slope: float32 [128, 512], replicated
- exit_matrix_slope: float32 [512, 512], replicated
- blend_matrix_slope: float32 [512, 512], replicated
- observation_slope: bfloat16 [131072, 128], P(('enc', 'blk'))
Inputs may be any that keep to these rules, and one draw needn't show every extreme that they name: In every draw some cycle r has live_count[r, s] = 2 for every source s.
All inputs are finite; a program needn't handle non-finite values.
Results may differ from a plain program's by a relative error of at most 0.0095.
Values may be sent and summed in bfloat16 or wider, within the bound.
No kernel may reach another device: no remote copies, remote signals or barrier semaphores. Data moves between devices by JAX's collectives and lax.ppermute only.
A program may use at most 64 MiB of HBM per device.

v0:
```python
import math
import jax
import jax.numpy as jnp
from jax import lax
from jax.sharding import PartitionSpec as P

CODE_BREADTH = 512
LON = 1440
MODES = 128
CAP = 2


def extended(block, sides, width):
    for axis, dim in sides:
        count = lax.axis_size(axis)
        forward = [(i, i + 1) for i in range(count - 1)]
        backward = [(target, source) for source, target in forward]
        low = lax.ppermute(
            lax.slice_in_dim(block, block.shape[dim] - width, None, axis=dim), axis, forward
        )
        high = lax.ppermute(lax.slice_in_dim(block, 0, width, axis=dim), axis, backward)
        block = jnp.concatenate([low, block, high], axis=dim)
    return block


def from_behind(value, axis, steps):
    count = lax.axis_size(axis)
    initial, last = (max(0, -steps), min(count, count - steps))
    return lax.ppermute(value, axis, [(source, source + steps) for source in range(initial, last)])


def tables():
    wavenum = jnp.arange(MODES, dtype=jnp.int32)
    lon_pos = jnp.arange(LON, dtype=jnp.int32)
    phases = (wavenum[:, None] * lon_pos[None, :] % LON).astype(jnp.float32) * (2.0 * math.pi / LON)
    forward = jnp.concatenate([jnp.cos(phases), -jnp.sin(phases)], 0).astype(jnp.bfloat16)
    weight = jnp.where(wavenum == 0, 1.0, 2.0).astype(jnp.float32) / LON
    inverse = jnp.concatenate(
        [jnp.cos(phases) * weight[:, None], -jnp.sin(phases) * weight[:, None]], 0
    ).T.astype(jnp.bfloat16)
    return (forward, inverse)


def silu_grad(values):
    logistic = jax.nn.sigmoid(values)
    return logistic * (1.0 + values * (1.0 - logistic))


def cell_table(lon_row, count_row):
    is_live = (jnp.arange(CAP, dtype=jnp.int32)[None, :] < count_row[:, None]).reshape(-1)
    matches = (lon_row[None, :] == jnp.arange(LON, dtype=jnp.int32)[:, None]) & is_live[None, :]
    return (matches.astype(jnp.bfloat16), jnp.sum(matches.astype(jnp.float32), axis=1))


def encode(rows, w_in, w_out):
    pre1 = jnp.dot(rows, w_in, preferred_element_type=jnp.float32)
    hidden = jax.nn.silu(pre1).astype(jnp.bfloat16)
    latent = jnp.dot(hidden, w_out, preferred_element_type=jnp.float32).astype(jnp.bfloat16)
    return (pre1, hidden, latent)


def encoder_grads(rows, pre1, hidden, grad_latent, w_in, w_out):
    out_local = jnp.dot(hidden.T, grad_latent, preferred_element_type=jnp.float32)
    grad_hidden = jnp.dot(grad_latent, w_out.T, preferred_element_type=jnp.float32)
    grad_pre1 = (grad_hidden * silu_grad(pre1)).astype(jnp.bfloat16)
    in_local = jnp.dot(rows.T, grad_pre1, preferred_element_type=jnp.float32)
    row_grads = jnp.dot(grad_pre1, w_in.T, preferred_element_type=jnp.float32).astype(jnp.bfloat16)
    return (in_local, out_local, row_grads)


def shards(
    observations, lon_index, live_count, w_in, w_out, w_spec, north, south, w_mix, loss_sensitivity
):
    enc_count = lax.axis_size("enc")
    blk_count = lax.axis_size("blk")
    devices = enc_count * blk_count
    slot_total = observations.shape[0]
    forward, inverse = tables()
    pre1, hidden, latent = encode(observations, w_in, w_out)
    outgoing = latent.reshape(enc_count, blk_count, CAP, CODE_BREADTH)
    arrived = lax.all_to_all(
        lax.all_to_all(outgoing, "enc", split_axis=0, concat_axis=0, tiled=True),
        "blk",
        split_axis=1,
        concat_axis=1,
        tiled=True,
    )
    lat_rows = arrived.reshape(slot_total, CODE_BREADTH)
    onehot, occupancy = cell_table(lon_index[0], live_count[0])
    denom = jnp.maximum(occupancy, 1.0)[:, None]
    grid_sum = jnp.dot(onehot, lat_rows, preferred_element_type=jnp.float32)
    resampled_field = (grid_sum / denom).astype(jnp.bfloat16)
    spectrum = jnp.dot(forward, resampled_field, preferred_element_type=jnp.float32)
    border = extended(resampled_field[None], ((("enc", "blk"), 0),), 1)
    spec_prev = jnp.dot(forward, border[0], preferred_element_type=jnp.float32)
    spec_next = jnp.dot(forward, border[2], preferred_element_type=jnp.float32)
    north_row = north[0][None, :]
    south_row = south[0][None, :]
    blended_fourier_modes = (
        spectrum * w_spec + north_row * spec_prev + south_row * spec_next
    ).astype(jnp.bfloat16)
    azimuth = jnp.dot(inverse, blended_fourier_modes, preferred_element_type=jnp.float32).astype(
        jnp.bfloat16
    )
    before_nonlinearity = jnp.dot(azimuth, w_mix, preferred_element_type=jnp.float32)
    predicted_state = (
        resampled_field.astype(jnp.float32) + jax.nn.silu(before_nonlinearity)
    ).astype(jnp.bfloat16)
    grad_pre = (loss_sensitivity[0].astype(jnp.float32) * silu_grad(before_nonlinearity)).astype(
        jnp.bfloat16
    )
    mix_local = jnp.dot(azimuth.T, grad_pre, preferred_element_type=jnp.float32)
    gridding_factor = 1.0 / math.sqrt(devices * LON)
    grad_az = jnp.dot(grad_pre, w_mix.T, preferred_element_type=jnp.float32).astype(jnp.bfloat16)
    blend_matrix_slope_local = jnp.dot(inverse.T, grad_az, preferred_element_type=jnp.float32)
    from_next = from_behind(north_row * blend_matrix_slope_local, ("enc", "blk"), -1)
    from_prev = from_behind(south_row * blend_matrix_slope_local, ("enc", "blk"), 1)
    grad_spec = (w_spec * blend_matrix_slope_local + from_next + from_prev).astype(jnp.bfloat16)
    grad_grid = loss_sensitivity[0].astype(jnp.float32) + jnp.dot(
        forward.T, grad_spec, preferred_element_type=jnp.float32
    )
    scaled = (grad_grid / denom).astype(jnp.bfloat16)
    grad_rows = jnp.dot(onehot.T, scaled, preferred_element_type=jnp.float32).astype(jnp.bfloat16)
    returned = lax.all_to_all(
        lax.all_to_all(
            grad_rows.reshape(enc_count, blk_count, CAP, CODE_BREADTH),
            "enc",
            split_axis=0,
            concat_axis=0,
            tiled=True,
        ),
        "blk",
        split_axis=1,
        concat_axis=1,
        tiled=True,
    )
    grad_latent = returned.reshape(slot_total, CODE_BREADTH)
    in_local, out_local, observation_slope = encoder_grads(
        observations, pre1, hidden, grad_latent, w_in, w_out
    )
    observed_factor = 1.0 / math.sqrt(devices * slot_total)
    input_gradient_total, output_gradient_total, blend_matrix_slope_summed = lax.psum(
        (in_local, out_local, mix_local), ("enc", "blk")
    )
    return (
        predicted_state[None],
        input_gradient_total * observed_factor,
        output_gradient_total * observed_factor,
        blend_matrix_slope_summed * gridding_factor,
        observation_slope,
    )


def solution(mesh):
    placed = (
        P(("enc", "blk"), None),
        P(("enc", "blk"), None),
        P(("enc", "blk"), None),
        P(),
        P(),
        P(),
        P(("enc", "blk"), None),
        P(("enc", "blk"), None),
        P(),
        P(("enc", "blk"), None, None),
    )
    return jax.shard_map(
        shards,
        mesh=mesh,
        in_specs=placed,
        out_specs=(P(("enc", "blk"), None, None), P(), P(), P(), P(("enc", "blk"), None)),
        check_vma=False,
    )
```

profile of v0, /device:TPU:8, one launch (start us, length us, event | category | flops | bytes accessed | tf_op | source)
XLA Modules:
  0.0 426.9 jit_solution(8997733929521939271)
XLA Ops:
  7.2 0.0 copy-start
  7.2 1.3 fusion.52
  8.5 0.0 copy-start.2
  8.5 1.0 copy-done.2
  9.5 1.5 convolution_convert_fusion.2
  11.0 0.2 reshape.48
  11.2 0.0 copy-start.11
  11.2 0.0 copy-start.19
  11.2 17.3 %all_to_all.20 = bf16[16,16,2,512]{3,2,1,0:T(2,128)(2,1)S(1)} all-to-all(bf16[16,16,2,512]{3,2,1,0:T(2,128)(2,1)S(1)} %reshape.48), channel_id=1, replica_groups=mesh['enc'=16,'blk'=16] {'enc'}, dimensions={0} | all-to-all | bytes 1048576 | tf_op jit(solution)/shard_map/all_to_all | solution.py:82
  28.5 1.3 copy.30
  29.8 8.6 %all-to-all-start.1 = ((bf16[16,16,2,512]{3,2,0,1:T(2,128)(2,1)}), bf16[16,16,2,512]{3,2,0,1:T(2,128)(2,1)S(1)}, u32[]{:S(2)}, u32[]{:S(2)}) async-start(bf16[16,16,2,512]{3,2,0,1:T(2,128)(2,1)} %copy.30), calls=%async_computation.1 | async-start | bytes 1048576 | tf_op jit(solution)/shard_map/all_to_all | solution.py:81
  38.4 0.0 copy-done.11
  38.4 0.1 iota_compare_fusion.1
  38.5 0.1 lt.38
  38.7 0.6 convert_reduce_fusion
  39.2 15.2 %all-to-all-done.1 = bf16[16,16,2,512]{3,2,0,1:T(2,128)(2,1)S(1)} async-done(((bf16[16,16,2,512]{3,2,0,1:T(2,128)(2,1)}), bf16[16,16,2,512]{3,2,0,1:T(2,128)(2,1)S(1)}, u32[]{:S(2)}, u32[]{:S(2)}) %all-to-all-start.1) | async-done | bytes 524320 | tf_op jit(solution)/shard_map/all_to_all | solution.py:81
  54.4 0.5 copy.31
  54.9 0.2 reshape.49
  55.1 1.0 divide_convert_fusion.1
  56.1 0.0 copy-start.12
  56.1 0.0 copy-start.14
  56.1 2.9 collective-permute-start.1
  59.1 2.7 collective-permute-start
  61.8 3.5 fusion.44
  65.3 4.1 multiply_convert_fusion.2
  69.4 0.0 copy-done.14
  69.4 1.4 convolution_multiply_fusion.1
  70.8 5.2 %collective-permute-done.1 = bf16[1,1440,512]{2,1,0:T(8,128)(2,1)S(1)} collective-permute-done((bf16[1,1440,512]{2,1,0:T(8,128)(2,1)S(1)}, bf16[1,1440,512]{2,1,0:T(8,128)(2,1)S(1)}, u32[]{:S(2)}, u32[]{:S(2)}) %collective-permute-start.1) | collective-permute-done | bytes 1474592 | tf_op jit(solution)/shard_map/ppermute | solution.py:21
  76.0 1.4 fusion.24
  77.3 4.6 %collective-permute-done = bf16[1,1440,512]{2,1,0:T(8,128)(2,1)S(1)} collective-permute-done((bf16[1,1440,512]{2,1,0:T(8,128)(2,1)S(1)}, bf16[1,1440,512]{2,1,0:T(8,128)(2,1)S(1)}, u32[]{:S(2)}, u32[]{:S(2)}) %collective-permute-start) | collective-permute-done | bytes 1474592 | tf_op jit(solution)/shard_map/ppermute | solution.py:18
  81.9 1.1 copy-done.13
  83.0 0.0 copy-done.18
  83.0 2.9 convolution_convert_fusion.1
  85.9 5.2 %fusion = (bf16[1440,512]{1,0:T(8,128)(2,1)S(1)}, bf16[1,1440,512]{2,1,0:T(8,128)(2,1)}) fusion(bf16[1,1440,512]{2,1,0:T(8,128)(2,1)} %param.19, bf16[1440,512]{1,0:T(8,128)(2,1)} %copy-done.12, bf16[1440,512]{1,0:T(8,128)(2,1)S(1)} %convolution_convert_fusion.1, bf16[512,512]{1,0:T(8,128)(2,1)S(1)} %copy-done), kind=kOutput, calls=%fused_computation.4 | convolution fusion | flops 765296640 | bytes 7897088 | tf_op jit(solution)/shard_map/dot_general | solution.py:105
  91.1 4.2 broadcast_multiply_fusion.3
  95.3 0.0 copy-done.1
  95.3 1.9 collective-permute-start.2
  97.2 2.6 collective-permute-start.3
  99.8 4.4 %collective-permute-done.2 = f32[256,512]{1,0:T(8,128)S(1)} collective-permute-done((f32[256,512]{1,0:T(8,128)}, f32[256,512]{1,0:T(8,128)S(1)}, u32[]{:S(2)}, u32[]{:S(2)}) %collective-permute-start.2) | collective-permute-done | bytes 524320 | tf_op jit(solution)/shard_map/ppermute | solution.py:29
  104.2 5.8 %collective-permute-done.3 = f32[256,512]{1,0:T(8,128)S(1)} collective-permute-done((f32[256,512]{1,0:T(8,128)}, f32[256,512]{1,0:T(8,128)S(1)}, u32[]{:S(2)}, u32[]{:S(2)}) %collective-permute-start.3) | collective-permute-done | bytes 524320 | tf_op jit(solution)/shard_map/ppermute | solution.py:29
  110.1 0.8 copy-done.16
  110.8 3.9 fusion.17
  114.7 0.2 reshape.50
  115.0 16.4 %all_to_all.21 = bf16[16,16,2,512]{3,2,1,0:T(2,128)(2,1)S(1)} all-to-all(bf16[16,16,2,512]{3,2,1,0:T(2,128)(2,1)S(1)} %reshape.50), channel_id=1, replica_groups=mesh['enc'=16,'blk'=16] {'enc'}, dimensions={0} | all-to-all | bytes 1048576 | tf_op jit(solution)/shard_map/all_to_all | solution.py:125
  131.3 1.3 copy.32
  132.6 3.6 all-to-all-start.3
  136.2 0.0 all-reduce.3.cloned.1.call-start
  136.2 3.3 fusion.53
  139.6 12.5 %all-to-all-done.3 = bf16[16,16,2,512]{3,2,0,1:T(2,128)(2,1)S(1)} async-done(((bf16[16,16,2,512]{3,2,0,1:T(2,128)(2,1)}), bf16[16,16,2,512]{3,2,0,1:T(2,128)(2,1)S(1)}, u32[]{:S(2)}, u32[]{:S(2)}) %all-to-all-start.3) | async-done | bytes 524320 | tf_op jit(solution)/shard_map/all_to_all | solution.py:124
  152.1 0.5 copy.33
  152.6 0.2 reshape.51
  152.8 0.0 copy-start.3
  152.8 2.0 fusion.20
  154.8 0.0 copy-done.3
  154.8 0.0 copy-start.6
  154.8 1.5 fusion.51
  156.3 1.0 convolution_bitcast_fusion
  157.3 0.0 all-reduce.3.cloned.1.call-update
  157.4 0.9 convolution_convert_fusion.3
  158.3 257.6 %all-reduce.3.cloned.1.call-done = (f32[128,512]{0,1:T(8,128)}, f32[512,512]{1,0:T(8,128)}, f32[512,512]{1,0:T(8,128)}) async-done(((f32[128,512]{0,1:T(8,128)}, f32[512,512]{1,0:T(8,128)}, f32[512,512]{1,0:T(8,128)}), (f32[128,512]{0,1:T(8,128)}, f32[512,512]{1,0:T(8,128)}, f32[512,512]{1,0:T(8,128)})) %all-reduce.3.cloned.1.call-update) | async-done | bytes 2359312 | tf_op jit(solution)/shard_map/psum | solution.py:142
  415.9 1.1 broadcast_multiply_fusion.4
  417.0 0.8 copy.34
  417.8 1.1 broadcast_multiply_fusion.1
  418.9 1.1 broadcast_multiply_fusion
  (26 shorter events, 0.1 us)
Async XLA Ops:
  7.2 78.7 %copy-start = (bf16[512,512]{1,0:T(8,128)(2,1)S(1)}, bf16[512,512]{1,0:T(8,128)(2,1)}, u32[]{:S(2)}) copy-start(bf16[512,512]{1,0:T(8,128)(2,1)} %param.18) | copy-start | bytes 1572868
  8.5 1.0 copy-start.2
  11.2 27.2 %copy-start.11 = (s32[1,256]{1,0:T(1,128)S(1)}, s32[1,256]{1,0:T(1,128)}, u32[]{:S(2)}) copy-start(s32[1,256]{1,0:T(1,128)} %param.12) | copy-start | bytes 3076
  11.2 27.5 %copy-start.19 = (s32[1,512]{1,0:T(1,128)S(1)}, s32[1,512]{1,0:T(1,128)}, u32[]{:S(2)}) copy-start(s32[1,512]{1,0:T(1,128)} %param.11) | copy-start | bytes 6148
  29.8 24.6 %all-to-all-start.1 = ((bf16[16,16,2,512]{3,2,0,1:T(2,128)(2,1)}), bf16[16,16,2,512]{3,2,0,1:T(2,128)(2,1)S(1)}, u32[]{:S(2)}, u32[]{:S(2)}) async-start(bf16[16,16,2,512]{3,2,0,1:T(2,128)(2,1)} %copy.30), calls=%async_computation.1 | async-start | bytes 1048576 | tf_op jit(solution)/shard_map/all_to_all | solution.py:81
  56.1 14.7 %copy-start.12 = (bf16[1440,512]{1,0:T(8,128)(2,1)}, bf16[1440,512]{1,0:T(8,128)(2,1)S(1)}, u32[]{:S(2)}) copy-start(bf16[1440,512]{1,0:T(8,128)(2,1)S(1)} %divide_convert_fusion.1) | copy-start | bytes 4423684
  56.1 13.3 %copy-start.14 = (f32[256,512]{1,0:T(8,128)S(1)}, f32[256,512]{1,0:T(8,128)}, u32[]{:S(2)}) copy-start(f32[256,512]{1,0:T(8,128)} %param.15) | copy-start | bytes 1572868
  56.1 19.8 %collective-permute-start.1 = (bf16[1,1440,512]{2,1,0:T(8,128)(2,1)S(1)}, bf16[1,1440,512]{2,1,0:T(8,128)(2,1)S(1)}, u32[]{:S(2)}, u32[]{:S(2)}) collective-permute-start(bf16[1,1440,512]{2,1,0:T(8,128)(2,1)S(1)} %bitcast.52), channel_id=1, source_target_pairs={{1,0},{2,1},{3,2},{4,3},{5,4},{6,5},{7,6},{8,7},{9,8},{10,9},{11,1... | collective-permute-start | bytes 4423688 | tf_op jit(solution)/shard_map/ppermute | solution.py:21
  59.1 22.8 %collective-permute-start = (bf16[1,1440,512]{2,1,0:T(8,128)(2,1)S(1)}, bf16[1,1440,512]{2,1,0:T(8,128)(2,1)S(1)}, u32[]{:S(2)}, u32[]{:S(2)}) collective-permute-start(bf16[1,1440,512]{2,1,0:T(8,128)(2,1)S(1)} %bitcast.53), channel_id=1, source_target_pairs={{0,1},{1,2},{2,3},{3,4},{4,5},{5,6},{6,7},{7,8},{8,9},{9,10},{10,1... | collective-permute-start | bytes 4423688 | tf_op jit(solution)/shard_map/ppermute | solution.py:18
  65.3 17.7 %copy-start.8 = (bf16[128,1440]{1,0:T(8,128)(2,1)}, bf16[128,1440]{1,0:T(8,128)(2,1)S(1)}, u32[]{:S(2)}) copy-start(bf16[128,1440]{1,0:T(8,128)(2,1)S(1)} %get-tuple-element.45) | copy-start | bytes 1105924
  65.3 17.7 %copy-start.9 = (bf16[128,1440]{1,0:T(8,128)(2,1)}, bf16[128,1440]{1,0:T(8,128)(2,1)S(1)}, u32[]{:S(2)}) copy-start(bf16[128,1440]{1,0:T(8,128)(2,1)S(1)} %get-tuple-element.46) | copy-start | bytes 1105924
  69.4 13.6 %copy-start.10 = (bf16[128,1440]{1,0:T(8,128)(2,1)}, bf16[128,1440]{1,0:T(8,128)(2,1)S(1)}, u32[]{:S(2)}) copy-start(bf16[128,1440]{1,0:T(8,128)(2,1)S(1)} %get-tuple-element.42) | copy-start | bytes 1105924
  69.4 6.5 %copy-start.17 = (f32[1,512]{1,0:T(1,128)S(1)}, f32[1,512]{1,0:T(1,128)}, u32[]{:S(2)}) copy-start(f32[1,512]{1,0:T(1,128)} %param.17) | copy-start | bytes 6148
  76.0 7.1 %copy-start.18 = (f32[1,512]{1,0:T(1,128)S(1)}, f32[1,512]{1,0:T(1,128)}, u32[]{:S(2)}) copy-start(f32[1,512]{1,0:T(1,128)} %param.16) | copy-start | bytes 6148
  81.9 1.1 copy-start.13
  91.1 4.2 copy-start.1
  95.3 8.9 %collective-permute-start.2 = (f32[256,512]{1,0:T(8,128)}, f32[256,512]{1,0:T(8,128)S(1)}, u32[]{:S(2)}, u32[]{:S(2)}) collective-permute-start(f32[256,512]{1,0:T(8,128)} %get-tuple-element.40), channel_id=1, source_target_pairs={{1,0},{2,1},{3,2},{4,3},{5,4},{6,5},{7,6},{8,7},{9,8},{10,9},{11,1... | collective-permute-start | bytes 1572872 | tf_op jit(solution)/shard_map/ppermute | solution.py:29
  97.2 12.8 %collective-permute-start.3 = (f32[256,512]{1,0:T(8,128)}, f32[256,512]{1,0:T(8,128)S(1)}, u32[]{:S(2)}, u32[]{:S(2)}) collective-permute-start(f32[256,512]{1,0:T(8,128)} %get-tuple-element.41), channel_id=1, source_target_pairs={{0,1},{1,2},{2,3},{3,4},{4,5},{5,6},{6,7},{7,8},{8,9},{9,10},{10,1... | collective-permute-start | bytes 1572872 | tf_op jit(solution)/shard_map/ppermute | solution.py:29
  110.1 0.8 copy-start.16
  132.6 19.5 %all-to-all-start.3 = ((bf16[16,16,2,512]{3,2,0,1:T(2,128)(2,1)}), bf16[16,16,2,512]{3,2,0,1:T(2,128)(2,1)S(1)}, u32[]{:S(2)}, u32[]{:S(2)}) async-start(bf16[16,16,2,512]{3,2,0,1:T(2,128)(2,1)} %copy.32), calls=%async_computation.3 | async-start | bytes 1048576 | tf_op jit(solution)/shard_map/all_to_all | solution.py:124
  136.2 279.7 %all-reduce.3.cloned.1.call-start = ((), (), s32[]{:S(2)}) async-start(), calls=%async_computation.4 | async-start | bytes 4718592 | tf_op jit(solution)/shard_map/psum | solution.py:142
  139.6 13.2 %copy-start.15 = (bf16[512,512]{1,0:T(8,128)(2,1)S(1)}, bf16[512,512]{1,0:T(8,128)(2,1)}, u32[]{:S(2)}) copy-start(bf16[512,512]{1,0:T(8,128)(2,1)} %param.14) | copy-start | bytes 1572868
  152.8 2.0 copy-start.3
  154.8 1.5 copy-start.6
  156.3 1.1 copy-start.7
  415.9 2.0 copy-start.5
  415.9 3.1 copy-start.4
Sparse Core Ops, SparseCore 0:
  157.5 258.3 all-reduce.2
where the time goes:
time: 428 us; the launch traced here: 427 us
  waiting for transfers between devices  305 us (71%)
  blocking collectives  33.7 us (8%)
  matrix products  31.5 us (7%)
  starting transfers between devices  22.3 us (5%)
  between operations  14.3 us (3%)
  other arithmetic  11.5 us (3%)
  local copies, waits for them, and re-layouts  8.33 us (2%)
    psum x1, waiting for transfers between devices, shards(): lax.psum((in_local, out_local, mix_local), ('enc', 'blk'))  258 us
    all_to_all x1, blocking collectives, shards(): lax.all_to_all(outgoing, 'enc', split_axis=0, concat_axis=0, tiled=True)  17.3 us
    all_to_all x1, blocking collectives, shards(): lax.all_to_all(grad_rows.reshape(enc_count, blk_count, CAP, CODE_BREADTH)...  16.4 us
    all_to_all x1, waiting for transfers between devices, shards(): lax.all_to_all(lax.all_to_all(outgoing, 'enc', split_axis=0, concat_axis=...  15.2 us
    all_to_all x1, waiting for transfers between devices, shards(): lax.all_to_all(lax.all_to_all(grad_rows.reshape(enc_count, blk_count, CAP...  12.5 us
    ppermute x2, waiting for transfers between devices, from_behind(): lax.ppermute(value, axis, [(source, source + steps) for source in range(i...  10.2 us
    all_to_all x1, starting transfers between devices, shards(): lax.all_to_all(lax.all_to_all(outgoing, 'enc', split_axis=0, concat_axis=...  8.58 us
  transfers between devices with their start and end apart: 7, of which 7 were waited for; matrix products, arithmetic and copies ran while one was open for 4% of the time, Pallas kernels for 0%

commit v1 on v0

--- a/solution.py
+++ b/solution.py
@@ -140,7 +140,7 @@
     )
     observed_factor = 1.0 / math.sqrt(devices * slot_total)
     input_gradient_total, output_gradient_total, blend_matrix_slope_summed = lax.psum(
-        (in_local, out_local, mix_local), ("enc", "blk")
+        lax.psum((in_local, out_local, mix_local), "enc"), "blk"
     )
     return (
         predicted_state[None],

time: 428 us -> 386 us (0.902)
  waiting for transfers between devices: 305 us -> 263 us
    psum x1 -> x2, waiting for transfers between devices: 258 us -> 216 us  [the longest x1 118 us: shards(): lax.psum(lax.psum((in_local, out_local, mix_local), 'enc'), 'blk')]
  transfers between devices with their start and end apart: 7 -> 8, of which waited for: 7 -> 8; matrix products, arithmetic and copies ran while one was open for 4% -> 4% of each run, Pallas kernels for 0% -> 0%
where the time goes in v1:
time: 386 us; the launch traced here: 385 us
  waiting for transfers between devices  263 us (68%)
  blocking collectives  33.7 us (9%)
  matrix products  31.5 us (8%)
  starting transfers between devices  22.4 us (6%)
  between operations  14.4 us (4%)
  other arithmetic  11.5 us (3%)
  local copies, waits for them, and re-layouts  8.33 us (2%)
    psum x1, waiting for transfers between devices, shards(): lax.psum(lax.psum((in_local, out_local, mix_local), 'enc'), 'blk')  118 us
    psum x1, waiting for transfers between devices, shards(): lax.psum((in_local, out_local, mix_local), 'enc')  97.7 us
    all_to_all x1, blocking collectives, shards(): lax.all_to_all(outgoing, 'enc', split_axis=0, concat_axis=0, tiled=True)  17.3 us
    all_to_all x1, blocking collectives, shards(): lax.all_to_all(grad_rows.reshape(enc_count, blk_count, CAP, CODE_BREADTH)...  16.4 us
    all_to_all x1, waiting for transfers between devices, shards(): lax.all_to_all(lax.all_to_all(outgoing, 'enc', split_axis=0, concat_axis=...  15.2 us
    all_to_all x1, waiting for transfers between devices, shards(): lax.all_to_all(lax.all_to_all(grad_rows.reshape(enc_count, blk_count, CAP...  12.5 us
    ppermute x2, waiting for transfers between devices, from_behind(): lax.ppermute(value, axis, [(source, source + steps) for source in range(i...  10.2 us
    all_to_all x1, starting transfers between devices, shards(): lax.all_to_all(lax.all_to_all(outgoing, 'enc', split_axis=0, concat_axis=...  8.58 us
  transfers between devices with their start and end apart: 8, of which 8 were waited for; matrix products, arithmetic and copies ran while one was open for 4% of the time, Pallas kernels for 0%

profile of v1, /device:TPU:8, one launch (start us, length us, event | category | flops | bytes accessed | tf_op | source)
XLA Modules:
  0.0 385.0 jit_solution(15690295101010344128)
XLA Ops:
  7.2 0.0 copy-start
  7.2 1.3 fusion.52
  8.5 0.0 copy-start.2
  8.5 1.0 copy-done.2
  9.5 1.5 convolution_convert_fusion.2
  11.0 0.2 reshape.48
  11.2 0.0 copy-start.11
  11.2 0.0 copy-start.19
  11.2 17.3 %all_to_all.20 = bf16[16,16,2,512]{3,2,1,0:T(2,128)(2,1)S(1)} all-to-all(bf16[16,16,2,512]{3,2,1,0:T(2,128)(2,1)S(1)} %reshape.48), channel_id=1, replica_groups=mesh['enc'=16,'blk'=16] {'enc'}, dimensions={0} | all-to-all | bytes 1048576 | tf_op jit(solution)/shard_map/all_to_all | solution.py:82
  28.5 1.3 copy.30
  29.8 8.6 %all-to-all-start.1 = ((bf16[16,16,2,512]{3,2,0,1:T(2,128)(2,1)}), bf16[16,16,2,512]{3,2,0,1:T(2,128)(2,1)S(1)}, u32[]{:S(2)}, u32[]{:S(2)}) async-start(bf16[16,16,2,512]{3,2,0,1:T(2,128)(2,1)} %copy.30), calls=%async_computation.1 | async-start | bytes 1048576 | tf_op jit(solution)/shard_map/all_to_all | solution.py:81
  38.4 0.0 copy-done.11
  38.4 0.1 iota_compare_fusion.1
  38.5 0.1 lt.38
  38.7 0.6 convert_reduce_fusion
  39.2 15.2 %all-to-all-done.1 = bf16[16,16,2,512]{3,2,0,1:T(2,128)(2,1)S(1)} async-done(((bf16[16,16,2,512]{3,2,0,1:T(2,128)(2,1)}), bf16[16,16,2,512]{3,2,0,1:T(2,128)(2,1)S(1)}, u32[]{:S(2)}, u32[]{:S(2)}) %all-to-all-start.1) | async-done | bytes 524320 | tf_op jit(solution)/shard_map/all_to_all | solution.py:81
  54.4 0.5 copy.31
  54.9 0.2 reshape.49
  55.1 1.0 divide_convert_fusion.1
  56.1 0.0 copy-start.12
  56.1 0.0 copy-start.14
  56.1 2.9 collective-permute-start.1
  59.1 2.7 collective-permute-start
  61.8 3.5 fusion.44
  65.3 4.1 %multiply_convert_fusion.2 = (bf16[128,1440]{1,0:T(8,128)(2,1)S(1)}, bf16[128,1440]{1,0:T(8,128)(2,1)}) fusion(f32[128]{0:T(128)S(1)} %fusion.48), kind=kLoop, calls=%fused_computation.45 | loop fusion | flops 2580480 | bytes 737792 | tf_op jit(solution)/shard_map/convert.3
  69.4 1.4 convolution_multiply_fusion.1
  70.8 5.1 %collective-permute-done.1 = bf16[1,1440,512]{2,1,0:T(8,128)(2,1)S(1)} collective-permute-done((bf16[1,1440,512]{2,1,0:T(8,128)(2,1)S(1)}, bf16[1,1440,512]{2,1,0:T(8,128)(2,1)S(1)}, u32[]{:S(2)}, u32[]{:S(2)}) %collective-permute-start.1) | collective-permute-done | bytes 1474592 | tf_op jit(solution)/shard_map/ppermute | solution.py:21
  76.0 1.4 fusion.24
  77.3 4.6 %collective-permute-done = bf16[1,1440,512]{2,1,0:T(8,128)(2,1)S(1)} collective-permute-done((bf16[1,1440,512]{2,1,0:T(8,128)(2,1)S(1)}, bf16[1,1440,512]{2,1,0:T(8,128)(2,1)S(1)}, u32[]{:S(2)}, u32[]{:S(2)}) %collective-permute-start) | collective-permute-done | bytes 1474592 | tf_op jit(solution)/shard_map/ppermute | solution.py:18
  81.9 1.1 copy-done.13
  83.1 2.9 convolution_convert_fusion.1
  85.9 5.2 %fusion = (bf16[1440,512]{1,0:T(8,128)(2,1)S(1)}, bf16[1,1440,512]{2,1,0:T(8,128)(2,1)}) fusion(bf16[1,1440,512]{2,1,0:T(8,128)(2,1)} %param.19, bf16[1440,512]{1,0:T(8,128)(2,1)} %copy-done.12, bf16[1440,512]{1,0:T(8,128)(2,1)S(1)} %convolution_convert_fusion.1, bf16[512,512]{1,0:T(8,128)(2,1)S(1)} %copy-done), kind=kOutput, calls=%fused_computation.4 | convolution fusion | flops 765296640 | bytes 7897088 | tf_op jit(solution)/shard_map/dot_general | solution.py:105
  91.1 4.2 %broadcast_multiply_fusion.3 = (f32[256,512]{1,0:T(8,128)}, f32[256,512]{1,0:T(8,128)}, f32[256,512]{1,0:T(8,128)}) fusion(f32[512]{0:T(512)S(1)} %bitcast.57, f32[512]{0:T(512)S(1)} %bitcast.55, bf16[1440,512]{1,0:T(8,128)(2,1)S(1)} %get-tuple-element.41, bf16[512,512]{1,0:T(8,128)(2,1)S(1)} %copy-done, bf16[128,1440]{1,0:T(8,128)(2,1)} %get-tuple-element.46, ...), kind=kOutput, calls=%fused_computation.57 | convolution fusion | flops 1134936064 | bytes 4313088 | tf_op jit(solution)/shard_map/dot_general | solution.py:115
  95.3 1.9 collective-permute-start.2
  97.2 2.6 collective-permute-start.3
  99.8 4.4 %collective-permute-done.2 = f32[256,512]{1,0:T(8,128)S(1)} collective-permute-done((f32[256,512]{1,0:T(8,128)}, f32[256,512]{1,0:T(8,128)S(1)}, u32[]{:S(2)}, u32[]{:S(2)}) %collective-permute-start.2) | collective-permute-done | bytes 524320 | tf_op jit(solution)/shard_map/ppermute | solution.py:29
  104.2 5.8 %collective-permute-done.3 = f32[256,512]{1,0:T(8,128)S(1)} collective-permute-done((f32[256,512]{1,0:T(8,128)}, f32[256,512]{1,0:T(8,128)S(1)}, u32[]{:S(2)}, u32[]{:S(2)}) %collective-permute-start.3) | collective-permute-done | bytes 524320 | tf_op jit(solution)/shard_map/ppermute | solution.py:29
  110.1 0.8 copy-done.16
  110.9 3.9 %fusion.17 = bf16[512,512]{1,0:T(8,128)(2,1)S(1)} fusion(s32[512]{0:T(512)S(1)} %bitcast.60, pred[512]{0:T(512)(128)(4,1)S(1)} %lt.38, bf16[1,1440,512]{2,1,0:T(8,128)(2,1)} %param.19, f32[1440]{0:T(1024)S(1)} %broadcast_maximum_fusion, f32[256,512]{1,0:T(8,128)} %copy-done.16, f32[256,512]{1,0:T(8,128)S(1)} %collective-permute-done.2, ...), kind=kOutput, calls=%fused_computation.24 | convolution fusion | flops 1139146752 | bytes 4841600 | tf_op jit(solution)/shard_map/dot_general | solution.py:123
  114.8 0.2 reshape.50
  115.0 16.4 %all_to_all.21 = bf16[16,16,2,512]{3,2,1,0:T(2,128)(2,1)S(1)} all-to-all(bf16[16,16,2,512]{3,2,1,0:T(2,128)(2,1)S(1)} %reshape.50), channel_id=1, replica_groups=mesh['enc'=16,'blk'=16] {'enc'}, dimensions={0} | all-to-all | bytes 1048576 | tf_op jit(solution)/shard_map/all_to_all | solution.py:125
  131.3 1.3 copy.32
  132.6 3.6 all-to-all-start.3
  136.2 0.0 all-reduce.7.cloned.1.call-start
  136.2 3.4 fusion.53
  139.6 12.5 %all-to-all-done.3 = bf16[16,16,2,512]{3,2,0,1:T(2,128)(2,1)S(1)} async-done(((bf16[16,16,2,512]{3,2,0,1:T(2,128)(2,1)}), bf16[16,16,2,512]{3,2,0,1:T(2,128)(2,1)S(1)}, u32[]{:S(2)}, u32[]{:S(2)}) %all-to-all-start.3) | async-done | bytes 524320 | tf_op jit(solution)/shard_map/all_to_all | solution.py:124
  152.1 0.5 copy.33
  152.6 0.2 reshape.51
  152.8 0.0 copy-start.3
  152.8 2.0 fusion.20
  154.8 0.0 copy-start.6
  154.8 1.5 fusion.51
  156.3 1.0 convolution_bitcast_fusion
  157.3 0.0 all-reduce.7.cloned.1.call-update
  157.4 0.0 copy-start.7
  157.4 0.0 all-reduce.5.cloned.1.call-start
  157.4 97.7 %all-reduce.7.cloned.1.call-done = (f32[128,512]{0,1:T(8,128)}, f32[512,512]{1,0:T(8,128)}, f32[512,512]{1,0:T(8,128)}) async-done(((f32[128,512]{0,1:T(8,128)}, f32[512,512]{1,0:T(8,128)}, f32[512,512]{1,0:T(8,128)}), (f32[128,512]{0,1:T(8,128)}, f32[512,512]{1,0:T(8,128)}, f32[512,512]{1,0:T(8,128)})) %all-reduce.7.cloned.1.call-update) | async-done | bytes 2359312 | tf_op jit(solution)/shard_map/psum | solution.py:143
  255.1 0.0 all-reduce.5.cloned.1.call-update
  255.2 1.0 convolution_convert_fusion.3
  256.1 117.9 %all-reduce.5.cloned.1.call-done = (f32[128,512]{0,1:T(8,128)}, f32[512,512]{1,0:T(8,128)}, f32[512,512]{1,0:T(8,128)}) async-done(((f32[128,512]{0,1:T(8,128)}, f32[512,512]{1,0:T(8,128)}, f32[512,512]{1,0:T(8,128)}), (f32[128,512]{0,1:T(8,128)}, f32[512,512]{1,0:T(8,128)}, f32[512,512]{1,0:T(8,128)})) %all-reduce.5.cloned.1.call-update) | async-done | bytes 2359312 | tf_op jit(solution)/shard_map/psum | solution.py:142
  374.0 1.1 broadcast_multiply_fusion.4
  375.1 0.8 copy.34
  376.0 1.1 broadcast_multiply_fusion.1
  377.1 1.1 broadcast_multiply_fusion
  (29 shorter events, 0.1 us)
Async XLA Ops:
  7.2 78.7 %copy-start = (bf16[512,512]{1,0:T(8,128)(2,1)S(1)}, bf16[512,512]{1,0:T(8,128)(2,1)}, u32[]{:S(2)}) copy-start(bf16[512,512]{1,0:T(8,128)(2,1)} %param.18) | copy-start | bytes 1572868
  8.5 1.0 copy-start.2
  11.2 27.2 %copy-start.11 = (s32[1,256]{1,0:T(1,128)S(1)}, s32[1,256]{1,0:T(1,128)}, u32[]{:S(2)}) copy-start(s32[1,256]{1,0:T(1,128)} %param.12) | copy-start | bytes 3076
  11.2 27.5 %copy-start.19 = (s32[1,512]{1,0:T(1,128)S(1)}, s32[1,512]{1,0:T(1,128)}, u32[]{:S(2)}) copy-start(s32[1,512]{1,0:T(1,128)} %param.11) | copy-start | bytes 6148
  29.8 24.6 %all-to-all-start.1 = ((bf16[16,16,2,512]{3,2,0,1:T(2,128)(2,1)}), bf16[16,16,2,512]{3,2,0,1:T(2,128)(2,1)S(1)}, u32[]{:S(2)}, u32[]{:S(2)}) async-start(bf16[16,16,2,512]{3,2,0,1:T(2,128)(2,1)} %copy.30), calls=%async_computation.1 | async-start | bytes 1048576 | tf_op jit(solution)/shard_map/all_to_all | solution.py:81
  56.1 14.7 %copy-start.12 = (bf16[1440,512]{1,0:T(8,128)(2,1)}, bf16[1440,512]{1,0:T(8,128)(2,1)S(1)}, u32[]{:S(2)}) copy-start(bf16[1440,512]{1,0:T(8,128)(2,1)S(1)} %divide_convert_fusion.1) | copy-start | bytes 4423684
  56.1 13.3 %copy-start.14 = (f32[256,512]{1,0:T(8,128)S(1)}, f32[256,512]{1,0:T(8,128)}, u32[]{:S(2)}) copy-start(f32[256,512]{1,0:T(8,128)} %param.15) | copy-start | bytes 1572868
  56.1 19.8 %collective-permute-start.1 = (bf16[1,1440,512]{2,1,0:T(8,128)(2,1)S(1)}, bf16[1,1440,512]{2,1,0:T(8,128)(2,1)S(1)}, u32[]{:S(2)}, u32[]{:S(2)}) collective-permute-start(bf16[1,1440,512]{2,1,0:T(8,128)(2,1)S(1)} %bitcast.52), channel_id=1, source_target_pairs={{1,0},{2,1},{3,2},{4,3},{5,4},{6,5},{7,6},{8,7},{9,8},{10,9},{11,1... | collective-permute-start | bytes 4423688 | tf_op jit(solution)/shard_map/ppermute | solution.py:21
  59.1 22.8 %collective-permute-start = (bf16[1,1440,512]{2,1,0:T(8,128)(2,1)S(1)}, bf16[1,1440,512]{2,1,0:T(8,128)(2,1)S(1)}, u32[]{:S(2)}, u32[]{:S(2)}) collective-permute-start(bf16[1,1440,512]{2,1,0:T(8,128)(2,1)S(1)} %bitcast.53), channel_id=1, source_target_pairs={{0,1},{1,2},{2,3},{3,4},{4,5},{5,6},{6,7},{7,8},{8,9},{9,10},{10,1... | collective-permute-start | bytes 4423688 | tf_op jit(solution)/shard_map/ppermute | solution.py:18
  65.3 17.7 %copy-start.8 = (bf16[128,1440]{1,0:T(8,128)(2,1)}, bf16[128,1440]{1,0:T(8,128)(2,1)S(1)}, u32[]{:S(2)}) copy-start(bf16[128,1440]{1,0:T(8,128)(2,1)S(1)} %get-tuple-element.48) | copy-start | bytes 1105924
  65.3 17.7 %copy-start.9 = (bf16[128,1440]{1,0:T(8,128)(2,1)}, bf16[128,1440]{1,0:T(8,128)(2,1)S(1)}, u32[]{:S(2)}) copy-start(bf16[128,1440]{1,0:T(8,128)(2,1)S(1)} %get-tuple-element.49) | copy-start | bytes 1105924
  69.4 13.6 %copy-start.10 = (bf16[128,1440]{1,0:T(8,128)(2,1)}, bf16[128,1440]{1,0:T(8,128)(2,1)S(1)}, u32[]{:S(2)}) copy-start(bf16[128,1440]{1,0:T(8,128)(2,1)S(1)} %get-tuple-element.45) | copy-start | bytes 1105924
  69.4 6.5 %copy-start.17 = (f32[1,512]{1,0:T(1,128)S(1)}, f32[1,512]{1,0:T(1,128)}, u32[]{:S(2)}) copy-start(f32[1,512]{1,0:T(1,128)} %param.17) | copy-start | bytes 6148
  76.0 7.1 %copy-start.18 = (f32[1,512]{1,0:T(1,128)S(1)}, f32[1,512]{1,0:T(1,128)}, u32[]{:S(2)}) copy-start(f32[1,512]{1,0:T(1,128)} %param.16) | copy-start | bytes 6148
  81.9 1.1 copy-start.13
  91.1 4.2 %copy-start.1 = (bf16[1440,512]{1,0:T(8,128)(2,1)}, bf16[1440,512]{1,0:T(8,128)(2,1)S(1)}, u32[]{:S(2)}) copy-start(bf16[1440,512]{1,0:T(8,128)(2,1)S(1)} %get-tuple-element.41) | copy-start | bytes 4423684
  95.3 8.9 %collective-permute-start.2 = (f32[256,512]{1,0:T(8,128)}, f32[256,512]{1,0:T(8,128)S(1)}, u32[]{:S(2)}, u32[]{:S(2)}) collective-permute-start(f32[256,512]{1,0:T(8,128)} %get-tuple-element.43), channel_id=1, source_target_pairs={{1,0},{2,1},{3,2},{4,3},{5,4},{6,5},{7,6},{8,7},{9,8},{10,9},{11,1... | collective-permute-start | bytes 1572872 | tf_op jit(solution)/shard_map/ppermute | solution.py:29
  97.2 12.8 %collective-permute-start.3 = (f32[256,512]{1,0:T(8,128)}, f32[256,512]{1,0:T(8,128)S(1)}, u32[]{:S(2)}, u32[]{:S(2)}) collective-permute-start(f32[256,512]{1,0:T(8,128)} %get-tuple-element.44), channel_id=1, source_target_pairs={{0,1},{1,2},{2,3},{3,4},{4,5},{5,6},{6,7},{7,8},{8,9},{9,10},{10,1... | collective-permute-start | bytes 1572872 | tf_op jit(solution)/shard_map/ppermute | solution.py:29
  110.1 0.8 copy-start.16
  132.6 19.5 %all-to-all-start.3 = ((bf16[16,16,2,512]{3,2,0,1:T(2,128)(2,1)}), bf16[16,16,2,512]{3,2,0,1:T(2,128)(2,1)S(1)}, u32[]{:S(2)}, u32[]{:S(2)}) async-start(bf16[16,16,2,512]{3,2,0,1:T(2,128)(2,1)} %copy.32), calls=%async_computation.3 | async-start | bytes 1048576 | tf_op jit(solution)/shard_map/all_to_all | solution.py:124
  136.2 118.9 %all-reduce.7.cloned.1.call-start = ((), (), s32[]{:S(2)}) async-start(), calls=%async_computation.5 | async-start | bytes 4718592 | tf_op jit(solution)/shard_map/psum | solution.py:143
  139.6 13.2 %copy-start.15 = (bf16[512,512]{1,0:T(8,128)(2,1)S(1)}, bf16[512,512]{1,0:T(8,128)(2,1)}, u32[]{:S(2)}) copy-start(bf16[512,512]{1,0:T(8,128)(2,1)} %param.14) | copy-start | bytes 1572868
  152.8 2.0 copy-start.3
  154.8 1.5 copy-start.6
  157.4 97.8 %copy-start.7 = (bf16[128,512]{1,0:T(8,128)(2,1)S(1)}, bf16[128,512]{1,0:T(8,128)(2,1)}, u32[]{:S(2)}) copy-start(bf16[128,512]{1,0:T(8,128)(2,1)} %param.13) | copy-start | bytes 393220
  157.4 216.6 %all-reduce.5.cloned.1.call-start = ((), (), s32[]{:S(2)}) async-start(), calls=%async_computation.4 | async-start | bytes 4718592 | tf_op jit(solution)/shard_map/psum | solution.py:142
  374.0 2.0 copy-start.5
  374.0 3.1 copy-start.4
Sparse Core Ops, SparseCore 0:
  157.5 97.6 all-reduce.6
  257.9 116.0 all-reduce.4
